TPU v7x, 768 devices: a whole 4x8x12 slice. The times are simulated.
768 devices in a mesh: dp: 192 (over y, z, core), proto: 4 (over x).
Axes of the slice: x: 4, y: 8, z: 12, core: 2. Of those that a mesh axis runs over, the one named last changes fastest.
Arguments:
- tokens: bfloat16 [24576, 256], P('dp'), may hold values from -48 to 48
- teacher_protos: float32 [4, 12288, 256], P('proto', 'dp'), may hold values from -48 to 48
- student_protos: float32 [4, 12288, 256], P('proto', 'dp'), may hold values from -48 to 48
- momentum: float32 [1], replicated, may hold values from 0.5 to 0.95
Outputs:
- teacher_next: float32 [4, 12288, 256], P('proto', 'dp')
- targets: bfloat16 [24576, 49152], P('dp', 'proto')
All inputs are finite; a program needn't handle non-finite values.
Results may differ from a plain program's by a relative error of at most 0.0054.
Values may be sent and summed in bfloat16 or wider, within the bound.
A program may use at most 32 MiB of HBM per device.

v0:
```python
import jax
import jax.numpy as jnp
from jax import lax
from jax.sharding import PartitionSpec as P

ITERS = 3


TEACHER_TEMP = 0.07


def unit_rows(matrix):
    return matrix / jnp.sqrt(jnp.sum(matrix * matrix, axis=-1, keepdims=True) + 1e-06)


def body(tokens, teacher_protos, student_protos, momentum):
    keep_rate = momentum[0]
    teacher_next = keep_rate * teacher_protos + (1.0 - keep_rate) * student_protos
    unit_protos = unit_rows(teacher_next).astype(jnp.bfloat16)
    unit_tokens = unit_rows(tokens.astype(jnp.float32)).astype(jnp.bfloat16)
    tok_count = unit_tokens.shape[0]
    group_width = teacher_next.shape[1] * lax.axis_size("dp")
    width_all = group_width * lax.axis_size("proto")
    gathered = lax.all_gather(unit_protos, "dp", axis=1, tiled=True)
    scores = lax.dot_general(
        unit_tokens, gathered[0], (((1,), (1,)), ((), ())), preferred_element_type=jnp.float32
    )
    base = jnp.exp(scores / TEACHER_TEMP)
    token_scale = jnp.ones((tok_count,), jnp.float32)
    proto_scale = jnp.ones((group_width,), jnp.float32)
    for repeat in range(ITERS):
        column_part = jnp.dot(token_scale, base, precision=lax.Precision.HIGHEST)
        proto_scale = 1.0 / lax.psum(column_part, "dp")
        row_part = jnp.dot(base, proto_scale, precision=lax.Precision.HIGHEST)
        token_scale = 1.0 / lax.psum(row_part, "proto")
    targets = ((width_all * token_scale)[:, None] * base * proto_scale[None, :]).astype(
        jnp.bfloat16
    )
    return (teacher_next, targets)


def solution(mesh):
    return jax.shard_map(
        body,
        mesh=mesh,
        in_specs=(P("dp", None), P("proto", "dp", None), P("proto", "dp", None), P()),
        out_specs=(P("proto", "dp", None), P("dp", "proto")),
        check_vma=False,
    )
```

profile of v0, /device:TPU:1, one launch (start us, length us, event | category | flops | bytes accessed | tf_op | source)
XLA Modules:
  0.0 2429.8 jit_solution(9853421715963570094)
XLA Ops:
  7.2 0.0 all-gather.2.cloned.1.call-start
  7.9 1.0 multiply_reduce_fusion
  8.8 0.0 copy-start.1
  8.9 0.7 divide_convert_fusion
  9.6 0.0 all-gather.2.cloned.1.call-update
  9.6 0.9 fusion.2
  10.6 134.4 %all-gather.2.cloned.1.call-done = bf16[1,12288,256]{2,1,0:T(8,128)(2,1)} async-done(((bf16[1,64,256]{2,1,0:T(8,128)(2,1)}), bf16[1,12288,256]{2,1,0:T(8,128)(2,1)}) %all-gather.2.cloned.1.call-update) | async-done | bytes 6291472 | tf_op jit(solution)/shard_map/all_gather | solution.py:24
  145.0 5.0 fusion
  150.0 0.0 copy-done.1
  150.0 0.0 copy-start
  150.1 2.7 copy-done
  152.7 3.0 fusion.12
  155.8 733.7 %psum.42 = f32[12288]{0:T(1024)S(1)} all-reduce(f32[12288]{0:T(1024)S(1)} %bitcast.38), channel_id=1, replica_groups=mesh['dp'=192,'proto'=4] {'dp'}, use_global_device_ids=true, to_apply=%region_2.0 | all-reduce | flops 12288 | bytes 98304 | tf_op jit(solution)/shard_map/psum | solution.py:33
  889.5 7.0 convolution_bitcast_fusion.2
  896.4 8.4 psum.43
  904.8 5.1 fusion.8
  909.9 737.6 %psum.44 = f32[12288]{0:T(1024)S(1)} all-reduce(f32[12288]{0:T(1024)S(1)} %bitcast.35), channel_id=1, replica_groups=mesh['dp'=192,'proto'=4] {'dp'}, use_global_device_ids=true, to_apply=%region_4.0 | all-reduce | flops 12288 | bytes 98304 | tf_op jit(solution)/shard_map/psum | solution.py:33
  1647.5 7.0 convolution_bitcast_fusion.1
  1654.5 6.2 psum.45
  1660.7 5.1 fusion.6
  1665.8 737.3 %psum.46 = f32[12288]{0:T(1024)S(1)} all-reduce(f32[12288]{0:T(1024)S(1)} %bitcast.37), channel_id=1, replica_groups=mesh['dp'=192,'proto'=4] {'dp'}, use_global_device_ids=true, to_apply=%region_6.0 | all-reduce | flops 12288 | bytes 98304 | tf_op jit(solution)/shard_map/psum | solution.py:33
  2403.1 7.0 convolution_bitcast_fusion
  2410.1 7.7 psum.47
  2417.8 5.2 multiply_convert_fusion
  (6 shorter events, 0.1 us)
Async XLA Ops:
  7.2 137.8 %all-gather.2.cloned.1.call-start = ((), (), s32[]{:S(2)}) async-start(), calls=%async_computation | async-start | bytes 6324224 | tf_op jit(solution)/shard_map/all_gather | solution.py:24
  8.8 141.2 %copy-start.1 = (f32[1,64,256]{2,1,0:T(8,128)}, f32[1,64,256]{2,1,0:T(8,128)S(1)}, u32[]{:S(2)}) copy-start(f32[1,64,256]{2,1,0:T(8,128)S(1)} %get-tuple-element.3) | copy-start | bytes 196612
  150.0 2.7 copy-start
Sparse Core Ops, SparseCore 0:
  12.3 132.6 all-gather.1
where the time goes:
time: 2440 us; the launch traced here: 2430 us
  blocking collectives  2230 us (91%)
  waiting for transfers between devices  134 us (5%)
  matrix products  39.1 us (2%)
    psum x3, blocking collectives, body(): proto_scale = 1.0 / lax.psum(column_part, 'dp')  2210 us
    all_gather x1, waiting for transfers between devices, body(): gathered = lax.all_gather(unit_protos, 'dp', axis=1, tiled=True)  134 us
  transfers between devices with their start and end apart: 1, of which 1 were waited for; matrix products, arithmetic and copies ran while one was open for 0% of the time, Pallas kernels for 0%

commit v1 on v0

v1 whole, which is shorter than its diff:
```python
import functools

import jax
import jax.numpy as jnp
from jax import lax
from jax.experimental import pallas as pl
from jax.experimental.pallas import tpu as pltpu
from jax.sharding import PartitionSpec as P

ITERS = 3
TEACHER_TEMP = 0.07
MESH = pl.DeviceIdType.MESH
F32 = jnp.float32
BF16 = jnp.bfloat16


def unit_rows(m):
    return m / jnp.sqrt(jnp.sum(m * m, axis=-1, keepdims=True) + 1e-06)


def nt_dot(a, b):
    return lax.dot_general(a, b, (((1,), (1,)), ((), ())), preferred_element_type=F32)


def two_term_rows(v):
    n = v.shape[1]
    x = jnp.broadcast_to(v, (16, n))
    hi = x.astype(BF16).astype(F32)
    row = lax.broadcasted_iota(jnp.int32, (16, n), 0)
    return jnp.where(row == 0, hi, jnp.where(row == 1, x - hi, 0.0)).astype(BF16)


def far_first(offsets, dist):
    return sorted(offsets, key=lambda o: (-dist(o), o))


def ring_dist(d, n):
    return min(d, n - d)


def sinkhorn_kernel(
    X, Y, Z,
    mom_ref, tok_ref, tea_ref, stu_ref,
    g_ref, ps_ref, ts_ref,
    pc, tc, base, csend, cpair, zbuf, rsend, xbuf, tbuf,
    own_sem, zg_send, zg_recv, tg_send, tg_recv, sf_send, sf_recv,
    c_send, c_recv, z_send, z_recv, r_send, r_recv, p_send, p_recv,
    ring_send, ring_recv, sib_send, sib_recv,
):
    x = lax.axis_index("proto")
    dp = lax.axis_index("dp")
    y, z, c = dp // (2 * Z), (dp // 2) % Z, dp % 2

    def at(xx, yy, zz, cc):
        return {"dp": (yy * Z + zz) * 2 + cc, "proto": xx}

    sibling = at(x, y, z, 1 - c)
    z_off = far_first(range(1, Z), lambda d: ring_dist(d, Z))
    y_off = far_first(range(1, Y), lambda d: ring_dist(d, Y))
    xy_off = far_first(
        [(dx, dy) for dx in range(X) for dy in range(Y) if (dx, dy) != (0, 0)],
        lambda o: ring_dist(o[0], X) + ring_dist(o[1], Y),
    )
    z_dev = [at(x, y, (z + d) % Z, c) for d in z_off]
    y_dev = [at(x, (y + d) % Y, z, c) for d in y_off]
    xy_dev = [at((x + dx) % X, (y + dy) % Y, z, c) for dx, dy in xy_off]

    barrier = pltpu.get_barrier_semaphore()
    greeted = [sibling] + z_dev + xy_dev
    for d in greeted:
        pl.semaphore_signal(barrier, inc=1, device_id=d, device_id_type=MESH)

    keep = mom_ref[0]
    pc[z, c] = unit_rows(keep * tea_ref[0] + (1.0 - keep) * stu_ref[0]).astype(BF16)
    tc[y] = unit_rows(tok_ref[...].astype(F32)).astype(BF16)
    pl.semaphore_wait(barrier, len(greeted))

    def send(src, dst, s, r, d):
        copy = pltpu.make_async_remote_copy(
            src_ref=src, dst_ref=dst, send_sem=s, recv_sem=r, device_id=d, device_id_type=MESH
        )
        copy.start()
        return copy

    def wait_bytes(ref, sem):
        pltpu.make_async_copy(ref, ref, sem).wait()

    for d in z_dev:
        send(pc.at[z, c], pc.at[z, c], zg_send, zg_recv, d)
    for d in y_dev:
        send(tc.at[y], tc.at[y], tg_send, tg_recv, d)
    wait_bytes(pc.at[0 : Z - 1, 0], zg_recv)
    swap = send(pc.at[:, c], pc.at[:, c], sf_send, sf_recv, sibling)

    up, down = at(x, (y + 1) % Y, z, c), at(x, (y + Y - 1) % Y, z, c)
    up_steps, down_steps = Y // 2, Y - 1 - Y // 2
    sends, sib = [], []

    def ring_step(s):
        if s <= up_steps:
            b = (y - s + 1 + Y) % Y
            src = pc.at[:, c] if s == 1 else g_ref.at[b, :, c]
            i = s - 1
            sends.append(send(src, g_ref.at[b, :, c], ring_send.at[i], ring_recv.at[i], up))
        if s <= down_steps:
            b = (y + s - 1) % Y
            src = pc.at[:, c] if s == 1 else g_ref.at[b, :, c]
            i = up_steps + s - 1
            sends.append(send(src, g_ref.at[b, :, c], ring_send.at[i], ring_recv.at[i], down))

    def ring_arrive(s):
        if s <= up_steps:
            b, i = (y - s + Y) % Y, s - 1
            wait_bytes(g_ref.at[b, :, c], ring_recv.at[i])
            sib.append(send(g_ref.at[b, :, c], g_ref.at[b, :, c], sib_send.at[i], sib_recv.at[i], sibling))
        if s <= down_steps:
            b, i = (y + s) % Y, up_steps + s - 1
            wait_bytes(g_ref.at[b, :, c], ring_recv.at[i])
            sib.append(send(g_ref.at[b, :, c], g_ref.at[b, :, c], sib_send.at[i], sib_recv.at[i], sibling))

    ring_step(1)
    wait_bytes(tc.at[0 : Y - 1], tg_recv)
    swap.wait_recv()
    own = pltpu.make_async_copy(pc, g_ref.at[y], own_sem)
    own.start()

    tdev = tc.shape[1]
    kb = base.shape[1]
    protos = pc[...].reshape(kb, pc.shape[3])

    def score(i, acc):
        b = jnp.exp(nt_dot(tc[i], protos) / TEACHER_TEMP)
        base[pl.ds(pl.multiple_of(i * tdev, tdev), tdev), :] = b.astype(BF16)
        return acc + jnp.sum(b, axis=0, keepdims=True)

    cols = lax.fori_loop(0, Y, score, jnp.zeros((1, kb), F32))

    for it in range(ITERS):
        csend[it, 0] = cols
        pair = send(csend.at[it, 0], cpair.at[it], c_send.at[it], c_recv.at[it], sibling)
        pair.wait_recv()
        cols = cols + cpair[it]
        csend[it, 1] = cols
        for i, d in enumerate(z_dev):
            send(csend.at[it, 1], zbuf.at[it, i], z_send.at[it], z_recv.at[it], d)
        wait_bytes(zbuf.at[it], z_recv.at[it])
        protos_scale = 1.0 / (cols + jnp.sum(zbuf[it], axis=0))
        if it == ITERS - 1:
            ps_ref[y] = protos_scale
            for d in y_dev:
                send(ps_ref.at[y], ps_ref.at[y], p_send, p_recv, d)
        rows = jnp.sum(nt_dot(two_term_rows(protos_scale), base[...]), axis=0, keepdims=True)
        rsend[it] = rows
        for i, d in enumerate(xy_dev):
            send(rsend.at[it], xbuf.at[it, i], r_send.at[it], r_recv.at[it], d)
        if 2 * it + 1 <= up_steps:
            ring_arrive(2 * it + 1)
            ring_step(2 * it + 2)
        wait_bytes(xbuf.at[it], r_recv.at[it])
        token_scale = 1.0 / (rows + jnp.sum(xbuf[it], axis=0))
        if it < ITERS - 1:
            cols = jnp.sum(
                jnp.dot(two_term_rows(token_scale), base[...], preferred_element_type=F32),
                axis=0,
                keepdims=True,
            )
            if 2 * it + 2 <= up_steps:
                ring_arrive(2 * it + 2)
                ring_step(2 * it + 3)
        else:
            for i in range(Y):
                tbuf[i] = token_scale[:, i * tdev : (i + 1) * tdev]
            ts_ref[...] = tbuf[y]
        pair.wait_send()
        wait_bytes(zbuf.at[it], z_send.at[it])
        wait_bytes(xbuf.at[it], r_send.at[it])

    wait_bytes(ps_ref.at[0 : Y - 1], p_recv)
    wait_bytes(ps_ref.at[0 : Y - 1], p_send)
    wait_bytes(pc.at[0 : Z - 1, 0], zg_send)
    wait_bytes(tc.at[0 : Y - 1], tg_send)
    own.wait()
    swap.wait_send()
    for copy in sends:
        copy.wait_send()
    for copy in sib:
        copy.wait()


def target_kernel(
    width, mom_ref, tok_ref, tea_ref, stu_ref, g_ref, ps_ref, ts_ref, next_ref, out_ref, unit, scale
):
    @pl.when(pl.program_id(0) == 0)
    def _():
        keep = mom_ref[0]
        next_ref[...] = keep * tea_ref[...] + (1.0 - keep) * stu_ref[...]
        unit[...] = unit_rows(tok_ref[...].astype(F32)).astype(BF16)
        n = ts_ref.shape[1]
        scale[...] = jnp.transpose(jnp.broadcast_to(width * ts_ref[...], (n, n)))

    b = jnp.exp(nt_dot(unit[...], g_ref[0]) / TEACHER_TEMP)
    out_ref[...] = (scale[:, 0:1] * b * ps_ref[0]).astype(BF16)


def body(X, Y, Z, tokens, teacher_protos, student_protos, momentum):
    tdev, width = tokens.shape
    kdev = teacher_protos.shape[1]
    kb, tb = 2 * Z * kdev, Y * tdev
    n_up = Y - 1
    dma = pltpu.SemaphoreType.DMA
    vmem = pl.BlockSpec(memory_space=pltpu.VMEM)
    smem = pl.BlockSpec(memory_space=pltpu.SMEM)
    groups, proto_scale, token_scale = pl.pallas_call(
        functools.partial(sinkhorn_kernel, X, Y, Z),
        out_shape=(
            jax.ShapeDtypeStruct((Y, Z, 2, kdev, width), BF16),
            jax.ShapeDtypeStruct((Y, 1, kb), F32),
            jax.ShapeDtypeStruct((1, tdev), F32),
        ),
        in_specs=[smem, vmem, vmem, vmem],
        out_specs=(pl.BlockSpec(memory_space=pl.ANY), vmem, vmem),
        scratch_shapes=[
            pltpu.VMEM((Z, 2, kdev, width), BF16),
            pltpu.VMEM((Y, tdev, width), BF16),
            pltpu.VMEM((tb, kb), BF16),
            pltpu.VMEM((ITERS, 2, 1, kb), F32),
            pltpu.VMEM((ITERS, 1, kb), F32),
            pltpu.VMEM((ITERS, Z - 1, 1, kb), F32),
            pltpu.VMEM((ITERS, 1, tb), F32),
            pltpu.VMEM((ITERS, X * Y - 1, 1, tb), F32),
            pltpu.VMEM((Y, 1, tdev), F32),
            dma, dma, dma, dma, dma, dma, dma,
            dma((ITERS,)), dma((ITERS,)), dma((ITERS,)), dma((ITERS,)), dma((ITERS,)), dma((ITERS,)),
            dma, dma,
            dma((n_up,)), dma((n_up,)), dma((n_up,)), dma((n_up,)),
        ],
        compiler_params=pltpu.CompilerParams(
            collective_id=0, has_side_effects=True, vmem_limit_bytes=40 * 2**20
        ),
        name="sinkhorn",
    )(momentum, tokens, teacher_protos, student_protos)
    groups = groups.reshape(Y, kb, width)
    return pl.pallas_call(
        functools.partial(target_kernel, float(X * Y * kb)),
        grid=(Y,),
        out_shape=(
            jax.ShapeDtypeStruct(teacher_protos.shape, F32),
            jax.ShapeDtypeStruct((tdev, Y * kb), BF16),
        ),
        in_specs=[
            smem,
            pl.BlockSpec((tdev, width), lambda i: (0, 0)),
            pl.BlockSpec((1, kdev, width), lambda i: (0, 0, 0)),
            pl.BlockSpec((1, kdev, width), lambda i: (0, 0, 0)),
            pl.BlockSpec((1, kb, width), lambda i: (i, 0, 0)),
            pl.BlockSpec((1, 1, kb), lambda i: (i, 0, 0)),
            pl.BlockSpec((1, tdev), lambda i: (0, 0)),
        ],
        out_specs=(
            pl.BlockSpec((1, kdev, width), lambda i: (0, 0, 0)),
            pl.BlockSpec((tdev, kb), lambda i: (0, i)),
        ),
        scratch_shapes=[pltpu.VMEM((tdev, width), BF16), pltpu.VMEM((tdev, tdev), F32)],
        compiler_params=pltpu.CompilerParams(vmem_limit_bytes=40 * 2**20),
        name="targets",
    )(momentum, tokens, teacher_protos, student_protos, groups, proto_scale, token_scale)


def build(mesh, X, Y, Z):
    return jax.shard_map(
        functools.partial(body, X, Y, Z),
        mesh=mesh,
        in_specs=(P("dp", None), P("proto", "dp", None), P("proto", "dp", None), P()),
        out_specs=(P("proto", "dp", None), P("dp", "proto")),
        check_vma=False,
    )


def solution(mesh):
    return build(mesh, mesh.shape["proto"], 8, mesh.shape["dp"] // 16)
```

time: 2440 us -> 106 us (0.04)
  blocking collectives: 2230 us -> 0 us
  waiting for transfers between devices: 134 us -> 0 us
  Pallas kernels: 0 us -> 102 us
  matrix products: 39.1 us -> 0 us
    psum x6 -> x0, blocking collectives: 2230 us -> none  [the longest x3 2210 us: body(): proto_scale = 1.0 / lax.psum(column_part, 'dp')]
    all_gather x1 -> x0, waiting for transfers between devices: 134 us -> none  [body(): gathered = lax.all_gather(unit_protos, 'dp', axis=1, tiled=True)]
    pallas_call x0 -> x2, Pallas kernels: none -> 102 us  [the longest x1 96.7 us: body(): pl.pallas_call(functools.partial(sinkhorn_kernel, X, Y, Z), out_shape=(ja...]
    dot_general x7 -> x0, matrix products: 39.1 us -> none  [the longest x3 20.9 us: body(): row_part = jnp.dot(base, proto_scale, precision=lax.Precision.HIGHEST)]
  transfers between devices with their start and end apart: 1 -> 0, of which waited for: 1 -> 0; matrix products, arithmetic and copies ran while one was open for 0% -> 0% of each run, Pallas kernels for 0% -> 0%
where the time goes in v1:
time: 106 us
  Pallas kernels  102 us (96%)
  local copies, waits for them, and re-layouts  2.51 us (2%)
  between operations  1.3 us (1%)
    pallas_call x1, Pallas kernels, body(): pl.pallas_call(functools.partial(sinkhorn_kernel, X, Y, Z), out_shape=(ja...  96.7 us
    pallas_call x1, Pallas kernels, body(): pl.pallas_call(functools.partial(target_kernel, float(X * Y * kb)), grid=...  5.26 us
    unnamed x6, local copies, waits for them, and re-layouts  2.51 us

profile of v1, /device:TPU:1, one launch (start us, length us, event | category | flops | bytes accessed | tf_op | source)
XLA Modules:
  0.0 105.7 jit_solution(9113973099302500166)
XLA Ops:
  1.3 0.0 copy-start
  1.3 0.8 copy-done
  2.1 0.0 copy-start.1
  2.1 0.8 copy-done.1
  3.0 0.0 copy-start.2
  3.0 0.8 copy-done.2
  3.8 96.7 %sinkhorn.1 = (bf16[8,12,2,64,256]{4,3,2,1,0:T(8,128)(2,1)S(1)}, f32[8,1,1536]{2,1,0:T(1,128)S(1)}, f32[1,128]{1,0:T(1,128)S(1)}) custom-call(f32[1]{0:T(128)S(6)} %copy.6.mom_ref, bf16[128,256]{1,0:T(8,128)(2,1)S(1)} %copy-done, f32[1,64,256]{2,1,0:T(8,128)S(1)} %copy-done.1, f32[1,64,256]{2,1,0:T(8,128)S(1)} %copy-done.2), custom_call_target="tpu_custom_call" | custom-call | tf_op jit(solution)/shard_map/sinkhorn/pallas_call | solution.py:213
  100.5 5.3 %targets.1 = (f32[1,64,256]{2,1,0:T(8,128)}, bf16[128,12288]{1,0:T(8,128)(2,1)}) custom-call(f32[1]{0:T(128)S(6)} %copy.6.mom_ref, bf16[128,256]{1,0:T(8,128)(2,1)S(1)} %copy-done, f32[1,64,256]{2,1,0:T(8,128)S(1)} %copy-done.1, f32[1,64,256]{2,1,0:T(8,128)S(1)} %copy-done.2, bf16[8,1536,256]{2,1,0:T(8,128)(2,1)S(1)} %bitcast.1, ...), custom_call_target="tpu_custom_call" | custom-call | tf_op jit(solution)/shard_map/targets/pallas_call | solution.py:243
Async XLA Ops:
  1.3 0.8 copy-start
  2.1 0.8 copy-start.1
  3.0 0.8 copy-start.2

commit v2 on v1

v2 whole, which is shorter than its diff:
```python
import functools

import jax
import jax.numpy as jnp
from jax import lax
from jax.experimental import pallas as pl
from jax.experimental.pallas import tpu as pltpu
from jax.sharding import PartitionSpec as P

ITERS = 3
TEACHER_TEMP = 0.07
MESH = pl.DeviceIdType.MESH
F32 = jnp.float32
BF16 = jnp.bfloat16


def unit_rows(m):
    return m / jnp.sqrt(jnp.sum(m * m, axis=-1, keepdims=True) + 1e-06)


def nt_dot(a, b):
    return lax.dot_general(a, b, (((1,), (1,)), ((), ())), preferred_element_type=F32)


def two_term_rows(v):
    n = v.shape[1]
    x = jnp.broadcast_to(v, (16, n))
    hi = x.astype(BF16).astype(F32)
    row = lax.broadcasted_iota(jnp.int32, (16, n), 0)
    return jnp.where(row == 0, hi, jnp.where(row == 1, x - hi, 0.0)).astype(BF16)


def far_first(offsets, dist):
    return sorted(offsets, key=lambda o: (-dist(o), o))


def ring_dist(d, n):
    return min(d, n - d)


def sinkhorn_kernel(
    X, Y, Z,
    mom_ref, tok_hbm, tea_hbm, stu_hbm,
    out_base, ps_ref, ts_ref, next_ref,
    tok_ref, tea_ref, stu_ref, g_ref, pc, tc, base, csend, cpair, zbuf, rsend, xbuf, tbuf,
    in_sem, zg_send, zg_recv, tg_send, tg_recv, sf_send, sf_recv,
    c_send, c_recv, z_send, z_recv, r_send, r_recv, p_send, p_recv,
    ring_send, ring_recv, sib_send, sib_recv,
):
    x = lax.axis_index("proto")
    dp = lax.axis_index("dp")
    y, z, c = dp // (2 * Z), (dp // 2) % Z, dp % 2

    def at(xx, yy, zz, cc):
        return {"dp": (yy * Z + zz) * 2 + cc, "proto": xx}

    sibling = at(x, y, z, 1 - c)
    z_off = far_first(range(1, Z), lambda d: ring_dist(d, Z))
    y_off = far_first(range(1, Y), lambda d: ring_dist(d, Y))
    xy_off = far_first(
        [(dx, dy) for dx in range(X) for dy in range(Y) if (dx, dy) != (0, 0)],
        lambda o: ring_dist(o[0], X) + ring_dist(o[1], Y),
    )
    z_dev = [at(x, y, (z + d) % Z, c) for d in z_off]
    y_dev = [at(x, (y + d) % Y, z, c) for d in y_off]
    xy_dev = [at((x + dx) % X, (y + dy) % Y, z, c) for dx, dy in xy_off]

    loads = [
        pltpu.make_async_copy(src, dst, in_sem.at[i])
        for i, (src, dst) in enumerate([(tea_hbm, tea_ref), (stu_hbm, stu_ref), (tok_hbm, tok_ref)])
    ]
    for load in loads:
        load.start()

    barrier = pltpu.get_barrier_semaphore()
    greeted = [sibling] + z_dev + xy_dev
    for d in greeted:
        pl.semaphore_signal(barrier, inc=1, device_id=d, device_id_type=MESH)

    keep = mom_ref[0]
    for load in loads:
        load.wait()
    teacher_next = keep * tea_ref[0] + (1.0 - keep) * stu_ref[0]
    next_ref[0] = teacher_next
    pc[z, c] = unit_rows(teacher_next).astype(BF16)
    tc[y] = unit_rows(tok_ref[...].astype(F32)).astype(BF16)
    pl.semaphore_wait(barrier, len(greeted))

    def send(src, dst, s, r, d):
        copy = pltpu.make_async_remote_copy(
            src_ref=src, dst_ref=dst, send_sem=s, recv_sem=r, device_id=d, device_id_type=MESH
        )
        copy.start()
        return copy

    def wait_bytes(ref, sem):
        pltpu.make_async_copy(ref, ref, sem).wait()

    for d in z_dev:
        send(pc.at[z, c], pc.at[z, c], zg_send, zg_recv, d)
    for d in y_dev:
        send(tc.at[y], tc.at[y], tg_send, tg_recv, d)
    wait_bytes(pc.at[0 : Z - 1, 0], zg_recv)
    swap = send(pc.at[:, c], pc.at[:, c], sf_send, sf_recv, sibling)

    up, down = at(x, (y + 1) % Y, z, c), at(x, (y + Y - 1) % Y, z, c)
    last, zh = Y // 2, Z // 2
    sends, sib = [], {}

    def ring_parts(s):
        if s < last:
            yield s - 1, up, (y - s + 1 + Y) % Y, (y - s + Y) % Y, slice(0, Z)
            yield last + s - 1, down, (y + s - 1) % Y, (y + s) % Y, slice(0, Z)
        elif s == last:
            yield s - 1, up, (y - s + 1 + Y) % Y, (y - s + Y) % Y, slice(0, zh)
            yield last + s - 1, down, (y + s - 1) % Y, (y + s) % Y, slice(zh, Z)

    def ring_step(s):
        for i, to, b, _, rows in ring_parts(s):
            src = pc.at[rows, c] if s == 1 else g_ref.at[b, rows, c]
            sends.append(send(src, g_ref.at[b, rows, c], ring_send.at[i], ring_recv.at[i], to))

    def ring_arrive(s):
        for i, _, _, b, rows in ring_parts(s):
            part = g_ref.at[b, rows, c]
            wait_bytes(part, ring_recv.at[i])
            sib[i] = send(part, part, sib_send.at[i], sib_recv.at[i], sibling)

    def ring_block(s):
        for i, _, _, b, _ in ring_parts(s):
            sib[i].wait_recv()
        for b in [(y - s + Y) % Y] * (s <= last) + [(y + s) % Y] * (s < last):
            block_base(b, g_ref[b])

    ring_step(1)
    wait_bytes(tc.at[0 : Y - 1], tg_recv)
    swap.wait_recv()

    tdev = tc.shape[1]
    kb = base.shape[1]
    protos = pc[...].reshape(kb, pc.shape[3])

    def block_base(b, block):
        scores = nt_dot(tc[y], block.reshape(kb, pc.shape[3]))
        out_base[b] = jnp.exp(scores / TEACHER_TEMP)

    def score(i, acc):
        b = jnp.exp(nt_dot(tc[i], protos) / TEACHER_TEMP)
        base[pl.ds(pl.multiple_of(i * tdev, tdev), tdev), :] = b.astype(BF16)
        return acc + jnp.sum(b, axis=0, keepdims=True)

    cols = lax.fori_loop(0, Y, score, jnp.zeros((1, kb), F32))

    for it in range(ITERS):
        csend[it, 0] = cols
        pair = send(csend.at[it, 0], cpair.at[it], c_send.at[it], c_recv.at[it], sibling)
        pair.wait_recv()
        cols = cols + cpair[it]
        csend[it, 1] = cols
        for i, d in enumerate(z_dev):
            send(csend.at[it, 1], zbuf.at[it, i], z_send.at[it], z_recv.at[it], d)
        if it == 0:
            block_base(y, pc[...])
        if it == 1:
            ring_block(1)
        if it == 2:
            ring_arrive(3)
            ring_step(4)
            ring_block(2)
        wait_bytes(zbuf.at[it], z_recv.at[it])
        protos_scale = 1.0 / (cols + jnp.sum(zbuf[it], axis=0))
        if it == ITERS - 1:
            ps_ref[y] = protos_scale
            for d in y_dev:
                send(ps_ref.at[y], ps_ref.at[y], p_send, p_recv, d)
        rows = jnp.sum(nt_dot(two_term_rows(protos_scale), base[...]), axis=0, keepdims=True)
        rsend[it] = rows
        for i, d in enumerate(xy_dev):
            send(rsend.at[it], xbuf.at[it, i], r_send.at[it], r_recv.at[it], d)
        if it == 1:
            ring_arrive(2)
            ring_step(3)
        if it == 2:
            ring_arrive(4)
            ring_block(3)
            ring_block(4)
        wait_bytes(xbuf.at[it], r_recv.at[it])
        token_scale = 1.0 / (rows + jnp.sum(xbuf[it], axis=0))
        if it < ITERS - 1:
            cols = jnp.sum(
                jnp.dot(two_term_rows(token_scale), base[...], preferred_element_type=F32),
                axis=0,
                keepdims=True,
            )
            if it == 0:
                ring_arrive(1)
                ring_step(2)
        else:
            for i in range(Y):
                tbuf[i] = token_scale[:, i * tdev : (i + 1) * tdev]
            ts_ref[...] = tbuf[y]
        pair.wait_send()
        wait_bytes(zbuf.at[it], z_send.at[it])
        wait_bytes(xbuf.at[it], r_send.at[it])

    wait_bytes(ps_ref.at[0 : Y - 1], p_recv)
    wait_bytes(ps_ref.at[0 : Y - 1], p_send)
    wait_bytes(pc.at[0 : Z - 1, 0], zg_send)
    wait_bytes(tc.at[0 : Y - 1], tg_send)
    swap.wait_send()
    for copy in sends:
        copy.wait_send()
    for copy in sib.values():
        copy.wait_send()


def target_kernel(width, new_ref, base_ref, ps_ref, ts_ref, next_ref, out_ref, scale):
    @pl.when(pl.program_id(0) == 0)
    def _():
        next_ref[...] = new_ref[...]
        n = ts_ref.shape[1]
        scale[...] = jnp.transpose(jnp.broadcast_to(width * ts_ref[...], (n, n)))

    out_ref[...] = (scale[:, 0:1] * base_ref[0] * ps_ref[0]).astype(BF16)


def body(X, Y, Z, tokens, teacher_protos, student_protos, momentum):
    tdev, width = tokens.shape
    kdev = teacher_protos.shape[1]
    kb, tb = 2 * Z * kdev, Y * tdev
    n_ring = 2 * (Y // 2)
    dma = pltpu.SemaphoreType.DMA
    vmem = pl.BlockSpec(memory_space=pltpu.VMEM)
    smem = pl.BlockSpec(memory_space=pltpu.SMEM)
    held = [
        pltpu.with_memory_space_constraint(v, pltpu.HBM)
        for v in (tokens, teacher_protos, student_protos)
    ]
    hbm = pl.BlockSpec(memory_space=pltpu.HBM)
    out_base, proto_scale, token_scale, teacher_next = pl.pallas_call(
        functools.partial(sinkhorn_kernel, X, Y, Z),
        out_shape=(
            jax.ShapeDtypeStruct((Y, tdev, kb), F32),
            jax.ShapeDtypeStruct((Y, 1, kb), F32),
            jax.ShapeDtypeStruct((1, tdev), F32),
            jax.ShapeDtypeStruct(teacher_protos.shape, F32),
        ),
        in_specs=[smem, hbm, hbm, hbm],
        out_specs=(vmem, vmem, vmem, vmem),
        scratch_shapes=[
            pltpu.VMEM((tdev, width), BF16),
            pltpu.VMEM((1, kdev, width), F32),
            pltpu.VMEM((1, kdev, width), F32),
            pltpu.VMEM((Y, Z, 2, kdev, width), BF16),
            pltpu.VMEM((Z, 2, kdev, width), BF16),
            pltpu.VMEM((Y, tdev, width), BF16),
            pltpu.VMEM((tb, kb), BF16),
            pltpu.VMEM((ITERS, 2, 1, kb), F32),
            pltpu.VMEM((ITERS, 1, kb), F32),
            pltpu.VMEM((ITERS, Z - 1, 1, kb), F32),
            pltpu.VMEM((ITERS, 1, tb), F32),
            pltpu.VMEM((ITERS, X * Y - 1, 1, tb), F32),
            pltpu.VMEM((Y, 1, tdev), F32),
            dma((3,)), dma, dma, dma, dma, dma, dma,
            dma((ITERS,)), dma((ITERS,)), dma((ITERS,)), dma((ITERS,)), dma((ITERS,)), dma((ITERS,)),
            dma, dma,
            dma((n_ring,)), dma((n_ring,)), dma((n_ring,)), dma((n_ring,)),
        ],
        compiler_params=pltpu.CompilerParams(
            collective_id=0, has_side_effects=True, vmem_limit_bytes=32 * 2**20
        ),
        name="sinkhorn",
    )(momentum, *held)
    return pl.pallas_call(
        functools.partial(target_kernel, float(X * Y * kb)),
        grid=(Y,),
        out_shape=(
            jax.ShapeDtypeStruct(teacher_protos.shape, F32),
            jax.ShapeDtypeStruct((tdev, Y * kb), BF16),
        ),
        in_specs=[
            pl.BlockSpec((1, kdev, width), lambda i: (0, 0, 0)),
            pl.BlockSpec((1, tdev, kb), lambda i: (i, 0, 0)),
            pl.BlockSpec((1, 1, kb), lambda i: (i, 0, 0)),
            pl.BlockSpec((1, tdev), lambda i: (0, 0)),
        ],
        out_specs=(
            pl.BlockSpec((1, kdev, width), lambda i: (0, 0, 0)),
            pl.BlockSpec((tdev, kb), lambda i: (0, i)),
        ),
        scratch_shapes=[pltpu.VMEM((tdev, tdev), F32)],
        compiler_params=pltpu.CompilerParams(vmem_limit_bytes=32 * 2**20),
        name="targets",
    )(teacher_next, out_base, proto_scale, token_scale)


def build(mesh, X, Y, Z):
    return jax.shard_map(
        functools.partial(body, X, Y, Z),
        mesh=mesh,
        in_specs=(P("dp", None), P("proto", "dp", None), P("proto", "dp", None), P()),
        out_specs=(P("proto", "dp", None), P("dp", "proto")),
        check_vma=False,
    )


def solution(mesh):
    return build(mesh, mesh.shape["proto"], 8, mesh.shape["dp"] // 16)
```

time: 106 us -> 92.3 us (0.87)
  Pallas kernels: 102 us -> 90.7 us
  local copies, waits for them, and re-layouts: 2.51 us -> 0 us
    pallas_call x1, Pallas kernels: 96.7 us -> 86.9 us  [body(): pl.pallas_call(functools.partial(sinkhorn_kernel, X, Y, Z), out_shape=(ja...]
    unnamed x6 -> x0, local copies, waits for them, and re-layouts: 2.51 us -> none
    pallas_call x1, Pallas kernels: 5.26 us -> 3.82 us  [body(): pl.pallas_call(functools.partial(target_kernel, float(X * Y * kb)), grid=...]
where the time goes in v2:
time: 92.3 us; the launch traced here: 92 us
  Pallas kernels  90.7 us (98%)
  between operations  1.28 us (1%)
    pallas_call x1, Pallas kernels, body(): pl.pallas_call(functools.partial(sinkhorn_kernel, X, Y, Z), out_shape=(ja...  86.9 us
    pallas_call x1, Pallas kernels, body(): pl.pallas_call(functools.partial(target_kernel, float(X * Y * kb)), grid=...  3.82 us

profile of v2, /device:TPU:1, one launch (start us, length us, event | category | flops | bytes accessed | tf_op | source)
XLA Modules:
  0.0 92.0 jit_solution(1778210147010609923)
XLA Ops:
  1.3 86.9 %sinkhorn.1 = (f32[8,128,1536]{2,1,0:T(8,128)S(1)}, f32[8,1,1536]{2,1,0:T(1,128)S(1)}, f32[1,128]{1,0:T(1,128)S(1)}, f32[1,64,256]{2,1,0:T(8,128)S(1)}) custom-call(f32[1]{0:T(128)S(6)} %copy.6.mom_ref, bf16[128,256]{1,0:T(8,128)(2,1)} %tok_hbm.1, f32[1,64,256]{2,1,0:T(8,128)} %tea_hbm.1, f32[1,64,256]{2,1,0:T(8,128)} %stu_hbm.1), custom_call_target="tpu_custom_call" | custom-call | tf_op jit(solution)/shard_map/sinkhorn/pallas_call | solution.py:240
  88.2 3.8 %targets.1 = (f32[1,64,256]{2,1,0:T(8,128)}, bf16[128,12288]{1,0:T(8,128)(2,1)}) custom-call(f32[1,64,256]{2,1,0:T(8,128)S(1)} %get-tuple-element.6.new_ref, f32[8,128,1536]{2,1,0:T(8,128)S(1)} %get-tuple-element.7.base_ref, f32[8,1,1536]{2,1,0:T(1,128)S(1)} %get-tuple-element.8.ps_ref, f32[1,128]{1,0:T(1,128)S(1)} %get-tuple-element.9.ts_ref), custom_call_target="tpu_custom_call" | custom-call | tf_op jit(solution)/shard_map/targets/pallas_call | solution.py:274

commit v3 on v2

--- a/solution.py
+++ b/solution.py
@@ -30,6 +30,18 @@
     return jnp.where(row == 0, hi, jnp.where(row == 1, x - hi, 0.0)).astype(BF16)
 
 
+def packed(v, rows):
+    n = v.shape[1] // 128
+    parts = [v[:, i * 128 : (i + 1) * 128] for i in range(n)]
+    if rows > n:
+        parts.append(jnp.zeros((rows - n, 128), v.dtype))
+    return jnp.concatenate(parts, axis=0)
+
+
+def unpacked(v, n):
+    return jnp.concatenate([v[i : i + 1] for i in range(n // 128)], axis=1)
+
+
 def far_first(offsets, dist):
     return sorted(offsets, key=lambda o: (-dist(o), o))
 
@@ -42,7 +54,7 @@
     X, Y, Z,
     mom_ref, tok_hbm, tea_hbm, stu_hbm,
     out_base, ps_ref, ts_ref, next_ref,
-    tok_ref, tea_ref, stu_ref, g_ref, pc, tc, base, csend, cpair, zbuf, rsend, xbuf, tbuf,
+    tok_ref, tea_ref, stu_ref, g_ref, pc, tc, base, csend, cpair, zsend, zbuf, rsend, xbuf, tbuf,
     in_sem, zg_send, zg_recv, tg_send, tg_recv, sf_send, sf_recv,
     c_send, c_recv, z_send, z_recv, r_send, r_recv, p_send, p_recv,
     ring_send, ring_recv, sib_send, sib_recv,
@@ -73,7 +85,12 @@
         load.start()
 
     barrier = pltpu.get_barrier_semaphore()
-    greeted = [sibling] + z_dev + xy_dev
+    far = lambda o: ring_dist(o[0], X) + ring_dist(o[1], Y) + ring_dist(o[2], Z)
+    offsets = [(0, 0, d) for d in z_off] + [(dx, dy, 0) for dx, dy in xy_off]
+    greeted = [
+        at((x + dx) % X, (y + dy) % Y, (z + dz) % Z, c)
+        for dx, dy, dz in sorted(offsets, key=lambda o: (-far(o), o))
+    ] + [sibling]
     for d in greeted:
         pl.semaphore_signal(barrier, inc=1, device_id=d, device_id_type=MESH)
 
@@ -96,10 +113,11 @@
     def wait_bytes(ref, sem):
         pltpu.make_async_copy(ref, ref, sem).wait()
 
-    for d in z_dev:
-        send(pc.at[z, c], pc.at[z, c], zg_send, zg_recv, d)
-    for d in y_dev:
-        send(tc.at[y], tc.at[y], tg_send, tg_recv, d)
+    for i in range(max(Z - 1, Y - 1)):
+        if i < Z - 1:
+            send(pc.at[z, c], pc.at[z, c], zg_send, zg_recv, z_dev[i])
+        if i < Y - 1:
+            send(tc.at[y], tc.at[y], tg_send, tg_recv, y_dev[i])
     wait_bytes(pc.at[0 : Z - 1, 0], zg_recv)
     swap = send(pc.at[:, c], pc.at[:, c], sf_send, sf_recv, sibling)
 
@@ -132,17 +150,18 @@
         for b in [(y - s + Y) % Y] * (s <= last) + [(y + s) % Y] * (s < last):
             block_base(b, g_ref[b])
 
+    tdev = tc.shape[1]
+    tb, kb = base.shape
+    width = pc.shape[3]
+
+    def block_base(b, block):
+        scores = nt_dot(tc[y], block.reshape(kb, width))
+        out_base[b] = jnp.exp(scores / TEACHER_TEMP)
+
     ring_step(1)
     wait_bytes(tc.at[0 : Y - 1], tg_recv)
     swap.wait_recv()
-
-    tdev = tc.shape[1]
-    kb = base.shape[1]
-    protos = pc[...].reshape(kb, pc.shape[3])
-
-    def block_base(b, block):
-        scores = nt_dot(tc[y], block.reshape(kb, pc.shape[3]))
-        out_base[b] = jnp.exp(scores / TEACHER_TEMP)
+    protos = pc[...].reshape(kb, width)
 
     def score(i, acc):
         b = jnp.exp(nt_dot(tc[i], protos) / TEACHER_TEMP)
@@ -151,14 +170,14 @@
 
     cols = lax.fori_loop(0, Y, score, jnp.zeros((1, kb), F32))
 
+    pairs = []
     for it in range(ITERS):
-        csend[it, 0] = cols
-        pair = send(csend.at[it, 0], cpair.at[it], c_send.at[it], c_recv.at[it], sibling)
+        csend[it] = packed(cols, csend.shape[1])
+        pair = send(csend.at[it], cpair.at[it], c_send.at[it], c_recv.at[it], sibling)
         pair.wait_recv()
-        cols = cols + cpair[it]
-        csend[it, 1] = cols
+        zsend[it] = (csend[it] + cpair[it]).astype(BF16)
         for i, d in enumerate(z_dev):
-            send(csend.at[it, 1], zbuf.at[it, i], z_send.at[it], z_recv.at[it], d)
+            send(zsend.at[it], zbuf.at[it, i], z_send.at[it], z_recv.at[it], d)
         if it == 0:
             block_base(y, pc[...])
         if it == 1:
@@ -168,24 +187,29 @@
             ring_step(4)
             ring_block(2)
         wait_bytes(zbuf.at[it], z_recv.at[it])
-        protos_scale = 1.0 / (cols + jnp.sum(zbuf[it], axis=0))
-        if it == ITERS - 1:
-            ps_ref[y] = protos_scale
-            for d in y_dev:
-                send(ps_ref.at[y], ps_ref.at[y], p_send, p_recv, d)
+        mass = zsend[it].astype(F32)
+        for i in range(Z - 1):
+            mass = mass + zbuf[it, i].astype(F32)
+        protos_scale = unpacked(1.0 / mass, kb)
         rows = jnp.sum(nt_dot(two_term_rows(protos_scale), base[...]), axis=0, keepdims=True)
-        rsend[it] = rows
+        rsend[it] = packed(rows, rsend.shape[1])
         for i, d in enumerate(xy_dev):
             send(rsend.at[it], xbuf.at[it, i], r_send.at[it], r_recv.at[it], d)
         if it == 1:
             ring_arrive(2)
             ring_step(3)
         if it == 2:
+            ps_ref[y] = protos_scale
+            for d in y_dev:
+                send(ps_ref.at[y], ps_ref.at[y], p_send, p_recv, d)
             ring_arrive(4)
             ring_block(3)
             ring_block(4)
         wait_bytes(xbuf.at[it], r_recv.at[it])
-        token_scale = 1.0 / (rows + jnp.sum(xbuf[it], axis=0))
+        mass = rsend[it]
+        for i in range(X * Y - 1):
+            mass = mass + xbuf[it, i]
+        token_scale = unpacked(1.0 / mass, tb)
         if it < ITERS - 1:
             cols = jnp.sum(
                 jnp.dot(two_term_rows(token_scale), base[...], preferred_element_type=F32),
@@ -199,12 +223,14 @@
             for i in range(Y):
                 tbuf[i] = token_scale[:, i * tdev : (i + 1) * tdev]
             ts_ref[...] = tbuf[y]
-        pair.wait_send()
+        pairs.append(pair)
+
+    wait_bytes(ps_ref.at[0 : Y - 1], p_recv)
+    wait_bytes(ps_ref.at[0 : Y - 1], p_send)
+    for it in range(ITERS):
+        pairs[it].wait_send()
         wait_bytes(zbuf.at[it], z_send.at[it])
         wait_bytes(xbuf.at[it], r_send.at[it])
-
-    wait_bytes(ps_ref.at[0 : Y - 1], p_recv)
-    wait_bytes(ps_ref.at[0 : Y - 1], p_send)
     wait_bytes(pc.at[0 : Z - 1, 0], zg_send)
     wait_bytes(tc.at[0 : Y - 1], tg_send)
     swap.wait_send()
@@ -214,20 +240,24 @@
         copy.wait_send()
 
 
-def target_kernel(width, new_ref, base_ref, ps_ref, ts_ref, next_ref, out_ref, scale):
-    @pl.when(pl.program_id(0) == 0)
-    def _():
-        next_ref[...] = new_ref[...]
-        n = ts_ref.shape[1]
-        scale[...] = jnp.transpose(jnp.broadcast_to(width * ts_ref[...], (n, n)))
-
-    out_ref[...] = (scale[:, 0:1] * base_ref[0] * ps_ref[0]).astype(BF16)
+def target_kernel(width, new_ref, base_ref, ps_ref, ts_ref, next_hbm, out_hbm, stage, sems):
+    blocks, n, kb = base_ref.shape
+    copies = [pltpu.make_async_copy(new_ref, next_hbm, sems.at[blocks])]
+    copies[0].start()
+    scale = jnp.transpose(jnp.broadcast_to(width * ts_ref[...], (n, n)))[:, 0:1]
+    for b in range(blocks):
+        stage[b] = (scale * base_ref[b] * ps_ref[b]).astype(BF16)
+        copies.append(pltpu.make_async_copy(stage.at[b], out_hbm.at[:, b * kb : (b + 1) * kb], sems.at[b]))
+        copies[-1].start()
+    for copy in copies:
+        copy.wait()
 
 
 def body(X, Y, Z, tokens, teacher_protos, student_protos, momentum):
     tdev, width = tokens.shape
     kdev = teacher_protos.shape[1]
     kb, tb = 2 * Z * kdev, Y * tdev
+    crows = -(-kb // 2048) * 16
     n_ring = 2 * (Y // 2)
     dma = pltpu.SemaphoreType.DMA
     vmem = pl.BlockSpec(memory_space=pltpu.VMEM)
@@ -255,11 +285,12 @@
             pltpu.VMEM((Z, 2, kdev, width), BF16),
             pltpu.VMEM((Y, tdev, width), BF16),
             pltpu.VMEM((tb, kb), BF16),
-            pltpu.VMEM((ITERS, 2, 1, kb), F32),
-            pltpu.VMEM((ITERS, 1, kb), F32),
-            pltpu.VMEM((ITERS, Z - 1, 1, kb), F32),
-            pltpu.VMEM((ITERS, 1, tb), F32),
-            pltpu.VMEM((ITERS, X * Y - 1, 1, tb), F32),
+            pltpu.VMEM((ITERS, crows, 128), F32),
+            pltpu.VMEM((ITERS, crows, 128), F32),
+            pltpu.VMEM((ITERS, crows, 128), BF16),
+            pltpu.VMEM((ITERS, Z - 1, crows, 128), BF16),
+            pltpu.VMEM((ITERS, tb // 128, 128), F32),
+            pltpu.VMEM((ITERS, X * Y - 1, tb // 128, 128), F32),
             pltpu.VMEM((Y, 1, tdev), F32),
             dma((3,)), dma, dma, dma, dma, dma, dma,
             dma((ITERS,)), dma((ITERS,)), dma((ITERS,)), dma((ITERS,)), dma((ITERS,)), dma((ITERS,)),
@@ -273,22 +304,13 @@
     )(momentum, *held)
     return pl.pallas_call(
         functools.partial(target_kernel, float(X * Y * kb)),
-        grid=(Y,),
         out_shape=(
             jax.ShapeDtypeStruct(teacher_protos.shape, F32),
             jax.ShapeDtypeStruct((tdev, Y * kb), BF16),
         ),
-        in_specs=[
-            pl.BlockSpec((1, kdev, width), lambda i: (0, 0, 0)),
-            pl.BlockSpec((1, tdev, kb), lambda i: (i, 0, 0)),
-            pl.BlockSpec((1, 1, kb), lambda i: (i, 0, 0)),
-            pl.BlockSpec((1, tdev), lambda i: (0, 0)),
-        ],
-        out_specs=(
-            pl.BlockSpec((1, kdev, width), lambda i: (0, 0, 0)),
-            pl.BlockSpec((tdev, kb), lambda i: (0, i)),
-        ),
-        scratch_shapes=[pltpu.VMEM((tdev, tdev), F32)],
+        in_specs=[vmem, vmem, vmem, vmem],
+        out_specs=(hbm, hbm),
+        scratch_shapes=[pltpu.VMEM((Y, tdev, kb), BF16), dma((Y + 1,))],
         compiler_params=pltpu.CompilerParams(vmem_limit_bytes=32 * 2**20),
         name="targets",
     )(teacher_next, out_base, proto_scale, token_scale)

time: 92.3 us -> 89.7 us (0.972)
  Pallas kernels: 90.7 us -> 88.2 us
    pallas_call x1, Pallas kernels: 3.82 us -> 1.99 us  [body(): pl.pallas_call(functools.partial(target_kernel, float(X * Y * kb)), out_s...]
where the time goes in v3:
time: 89.7 us; the launch traced here: 89.5 us
  Pallas kernels  88.2 us (98%)
  between operations  1.28 us (1%)
    pallas_call x1, Pallas kernels, body(): pl.pallas_call(functools.partial(sinkhorn_kernel, X, Y, Z), out_shape=(ja...  86.2 us
    pallas_call x1, Pallas kernels, body(): pl.pallas_call(functools.partial(target_kernel, float(X * Y * kb)), out_s...  1.99 us

profile of v3, /device:TPU:1, one launch (start us, length us, event | category | flops | bytes accessed | tf_op | source)
XLA Modules:
  0.0 89.5 jit_solution(1787854653123447007)
XLA Ops:
  1.3 86.2 %sinkhorn.1 = (f32[8,128,1536]{2,1,0:T(8,128)S(1)}, f32[8,1,1536]{2,1,0:T(1,128)S(1)}, f32[1,128]{1,0:T(1,128)S(1)}, f32[1,64,256]{2,1,0:T(8,128)S(1)}) custom-call(f32[1]{0:T(128)S(6)} %copy.6.mom_ref, bf16[128,256]{1,0:T(8,128)(2,1)} %tok_hbm.1, f32[1,64,256]{2,1,0:T(8,128)} %tea_hbm.1, f32[1,64,256]{2,1,0:T(8,128)} %stu_hbm.1), custom_call_target="tpu_custom_call" | custom-call | tf_op jit(solution)/shard_map/sinkhorn/pallas_call | solution.py:270
  87.5 2.0 %targets.1 = (f32[1,64,256]{2,1,0:T(8,128)}, bf16[128,12288]{1,0:T(8,128)(2,1)}) custom-call(f32[1,64,256]{2,1,0:T(8,128)S(1)} %get-tuple-element.6.new_ref, f32[8,128,1536]{2,1,0:T(8,128)S(1)} %get-tuple-element.7.base_ref, f32[8,1,1536]{2,1,0:T(1,128)S(1)} %get-tuple-element.8.ps_ref, f32[1,128]{1,0:T(1,128)S(1)} %get-tuple-element.9.ts_ref), custom_call_target="tpu_custom_call" | custom-call | tf_op jit(solution)/shard_map/targets/pallas_call | solution.py:305

commit v4 on v3

--- a/solution.py
+++ b/solution.py
@@ -163,12 +163,9 @@
     swap.wait_recv()
     protos = pc[...].reshape(kb, width)
 
-    def score(i, acc):
-        b = jnp.exp(nt_dot(tc[i], protos) / TEACHER_TEMP)
-        base[pl.ds(pl.multiple_of(i * tdev, tdev), tdev), :] = b.astype(BF16)
-        return acc + jnp.sum(b, axis=0, keepdims=True)
-
-    cols = lax.fori_loop(0, Y, score, jnp.zeros((1, kb), F32))
+    b = jnp.exp(nt_dot(tc[...].reshape(tb, width), protos) / TEACHER_TEMP)
+    base[...] = b.astype(BF16)
+    cols = jnp.sum(b, axis=0, keepdims=True)
 
     pairs = []
     for it in range(ITERS):
@@ -183,9 +180,9 @@
         if it == 1:
             ring_block(1)
         if it == 2:
+            ring_block(2)
             ring_arrive(3)
             ring_step(4)
-            ring_block(2)
         wait_bytes(zbuf.at[it], z_recv.at[it])
         mass = zsend[it].astype(F32)
         for i in range(Z - 1):
@@ -202,8 +199,8 @@
             ps_ref[y] = protos_scale
             for d in y_dev:
                 send(ps_ref.at[y], ps_ref.at[y], p_send, p_recv, d)
+            ring_block(3)
             ring_arrive(4)
-            ring_block(3)
             ring_block(4)
         wait_bytes(xbuf.at[it], r_recv.at[it])
         mass = rsend[it]

time: 89.7 us -> 87.3 us (0.973)
  Pallas kernels: 88.2 us -> 85.8 us
    pallas_call x1, Pallas kernels: 86.2 us -> 83.8 us  [body(): pl.pallas_call(functools.partial(sinkhorn_kernel, X, Y, Z), out_shape=(ja...]
where the time goes in v4:
time: 87.3 us; the launch traced here: 87.1 us
  Pallas kernels  85.8 us (98%)
  between operations  1.28 us (1%)
    pallas_call x1, Pallas kernels, body(): pl.pallas_call(functools.partial(sinkhorn_kernel, X, Y, Z), out_shape=(ja...  83.8 us
    pallas_call x1, Pallas kernels, body(): pl.pallas_call(functools.partial(target_kernel, float(X * Y * kb)), out_s...  1.99 us

profile of v4, /device:TPU:1, one launch (start us, length us, event | category | flops | bytes accessed | tf_op | source)
XLA Modules:
  0.0 87.1 jit_solution(8744698802433698646)
XLA Ops:
  1.3 83.8 %sinkhorn.1 = (f32[8,128,1536]{2,1,0:T(8,128)S(1)}, f32[8,1,1536]{2,1,0:T(1,128)S(1)}, f32[1,128]{1,0:T(1,128)S(1)}, f32[1,64,256]{2,1,0:T(8,128)S(1)}) custom-call(f32[1]{0:T(128)S(6)} %copy.6.mom_ref, bf16[128,256]{1,0:T(8,128)(2,1)} %tok_hbm.1, f32[1,64,256]{2,1,0:T(8,128)} %tea_hbm.1, f32[1,64,256]{2,1,0:T(8,128)} %stu_hbm.1), custom_call_target="tpu_custom_call" | custom-call | tf_op jit(solution)/shard_map/sinkhorn/pallas_call | solution.py:267
  85.1 2.0 %targets.1 = (f32[1,64,256]{2,1,0:T(8,128)}, bf16[128,12288]{1,0:T(8,128)(2,1)}) custom-call(f32[1,64,256]{2,1,0:T(8,128)S(1)} %get-tuple-element.6.new_ref, f32[8,128,1536]{2,1,0:T(8,128)S(1)} %get-tuple-element.7.base_ref, f32[8,1,1536]{2,1,0:T(1,128)S(1)} %get-tuple-element.8.ps_ref, f32[1,128]{1,0:T(1,128)S(1)} %get-tuple-element.9.ts_ref), custom_call_target="tpu_custom_call" | custom-call | tf_op jit(solution)/shard_map/targets/pallas_call | solution.py:302

commit v5 on v4

--- a/solution.py
+++ b/solution.py
@@ -1,4 +1,5 @@
 import functools
+import math
 
 import jax
 import jax.numpy as jnp
@@ -9,6 +10,7 @@
 
 ITERS = 3
 TEACHER_TEMP = 0.07
+EXP2_RATE = math.log2(math.e) / TEACHER_TEMP
 MESH = pl.DeviceIdType.MESH
 F32 = jnp.float32
 BF16 = jnp.bfloat16
@@ -156,14 +158,14 @@
 
     def block_base(b, block):
         scores = nt_dot(tc[y], block.reshape(kb, width))
-        out_base[b] = jnp.exp(scores / TEACHER_TEMP)
+        out_base[b] = jnp.exp2(scores * EXP2_RATE)
 
     ring_step(1)
     wait_bytes(tc.at[0 : Y - 1], tg_recv)
     swap.wait_recv()
     protos = pc[...].reshape(kb, width)
 
-    b = jnp.exp(nt_dot(tc[...].reshape(tb, width), protos) / TEACHER_TEMP)
+    b = jnp.exp2(nt_dot(tc[...].reshape(tb, width), protos) * EXP2_RATE)
     base[...] = b.astype(BF16)
     cols = jnp.sum(b, axis=0, keepdims=True)
 

time: 87.3 us -> 87.1 us (level)
  no operation moved by 1% of the time
where the time goes in v5:
time: 87.1 us; the launch traced here: 86.9 us
  Pallas kernels  85.6 us (98%)
  between operations  1.28 us (1%)
    pallas_call x1, Pallas kernels, body(): pl.pallas_call(functools.partial(sinkhorn_kernel, X, Y, Z), out_shape=(ja...  83.6 us
    pallas_call x1, Pallas kernels, body(): pl.pallas_call(functools.partial(target_kernel, float(X * Y * kb)), out_s...  1.99 us

profile of v5, /device:TPU:1, one launch (start us, length us, event | category | flops | bytes accessed | tf_op | source)
XLA Modules:
  0.0 86.9 jit_solution(4014757596147867027)
XLA Ops:
  1.3 83.6 %sinkhorn.1 = (f32[8,128,1536]{2,1,0:T(8,128)S(1)}, f32[8,1,1536]{2,1,0:T(1,128)S(1)}, f32[1,128]{1,0:T(1,128)S(1)}, f32[1,64,256]{2,1,0:T(8,128)S(1)}) custom-call(f32[1]{0:T(128)S(6)} %copy.6.mom_ref, bf16[128,256]{1,0:T(8,128)(2,1)} %tok_hbm.1, f32[1,64,256]{2,1,0:T(8,128)} %tea_hbm.1, f32[1,64,256]{2,1,0:T(8,128)} %stu_hbm.1), custom_call_target="tpu_custom_call" | custom-call | tf_op jit(solution)/shard_map/sinkhorn/pallas_call | solution.py:269
  84.9 2.0 %targets.1 = (f32[1,64,256]{2,1,0:T(8,128)}, bf16[128,12288]{1,0:T(8,128)(2,1)}) custom-call(f32[1,64,256]{2,1,0:T(8,128)S(1)} %get-tuple-element.6.new_ref, f32[8,128,1536]{2,1,0:T(8,128)S(1)} %get-tuple-element.7.base_ref, f32[8,1,1536]{2,1,0:T(1,128)S(1)} %get-tuple-element.8.ps_ref, f32[1,128]{1,0:T(1,128)S(1)} %get-tuple-element.9.ts_ref), custom_call_target="tpu_custom_call" | custom-call | tf_op jit(solution)/shard_map/targets/pallas_call | solution.py:304
